TPU v7x, 512 devices: a whole 4x8x8 slice. The times are simulated.
512 devices in a mesh: member: 16 (over z_lo, y), space: 32 (over z_hi, x, core).
Axes of the slice: x: 4, y: 8, z: 8 (z_hi: 4, z_lo: 2; z = z_hi * 2 + z_lo), core: 2. Of those that a mesh axis runs over, the one named last changes fastest.
Arguments:
- ensemble: float32 [64, 512, 2048], P('member', 'space'), may hold values from -6 to 6
- spreading_number: float32 [512, 2048], P('space'), may hold values from 0.05 to 0.2
- zonal_transport_ratio: float32 [512, 2048], P('space'), may hold values from -0.2 to 0.2
- meridional_transport_ratio: float32 [512, 2048], P('space'), may hold values from -0.2 to 0.2
- ocean_mask: int32 [512, 2048], P('space'), may hold values 0 or 1
- obs_loc: int32 [65536], replicated, may hold values from 0 to 1048575, as said below
- obs_value: float32 [65536], replicated, may hold values from -6 to 6
- obs_sigma: float32 [65536], replicated, may hold values from 0.3 to 1
- tile_obs: int32 [512, 16, 256], P('space'), may hold values from 0 to 65535, as said below
Outputs:
- analysis: float32 [64, 512, 2048], P('member', 'space')
Inputs may be any that keep to these rules, and one draw needn't show every extreme that they name: `obs_loc`: observation j lies in grid rows (j // 2048) * 16 to (j // 2048 + 1) * 16 - 1. `tile_obs`: the observations named for a tile in grid row r have indices from (r // 16 - 1) * 2048 to (r // 16 + 2) * 2048 - 1; repeats may occur.
All inputs are finite; a program needn't handle non-finite values. No bound on the sum of `ocean_mask` on one device may be relied on, other than what follows from the above.
Results may differ from a plain program's by a relative error of at most 0.0003.
Values sent between devices are 32-bit elements; how exact they have to be, the bound alone decides.
A program may use at most 64 MiB of HBM per device.

v0:
```python
import jax
import jax.numpy as jnp
from jax import lax
from jax.sharding import PartitionSpec as P

TILE_COLS = 128
LOC_RADIUS = 96
NS_ITERS = 6


highest = lax.Precision.HIGHEST


def padded(cells, sides, width):
    for axis, dim in sides:
        count = lax.axis_size(axis)
        ends = count - 1
        head = lax.slice_in_dim(cells, 0, width, axis=dim)
        tail = lax.slice_in_dim(cells, cells.shape[dim] - width, cells.shape[dim], axis=dim)
        cells = jnp.concatenate(
            [
                lax.ppermute(tail, axis, [(i, (i + 1) % count) for i in range(ends)]),
                cells,
                lax.ppermute(head, axis, [((i + 1) % count, i) for i in range(ends)]),
            ],
            axis=dim,
        )
    return cells


def propagate_prior_state(
    haloed_state_grid,
    spreading_number,
    zonal_transport_ratio,
    meridional_transport_ratio,
    liquid_cell_flags,
):
    centre = haloed_state_grid[:, 1:-1, :]
    northern = haloed_state_grid[:, 2:, :]
    southern = haloed_state_grid[:, :-2, :]
    eastern = jnp.roll(centre, -1, axis=2)
    western = jnp.roll(centre, 1, axis=2)
    laplace = northern + southern + eastern + western - 4.0 * centre
    advect = (
        zonal_transport_ratio * (eastern - western) * 0.5
        + meridional_transport_ratio * (northern - southern) * 0.5
    )
    return liquid_cell_flags * (centre + spreading_number * laplace - advect)


def analyze(
    ensemble_block,
    anomalies,
    means,
    window_picks,
    global_picks,
    obs_loc,
    obs_value,
    obs_sigma,
    row_first,
    grid_cols,
):
    members, block_rows, block_cols = ensemble_block.shape
    tile_cols = block_cols // TILE_COLS
    tile_count = block_rows * tile_cols
    window_flat = window_picks.reshape(tile_count, -1)
    global_flat = global_picks.reshape(tile_count, -1)
    chosen = jnp.take(anomalies, window_flat, axis=1)
    chosen_mean = jnp.take(means, window_flat)
    location = jnp.take(obs_loc, global_flat)
    obs_row = location // grid_cols
    obs_col = location % grid_cols
    zero_grid = jnp.zeros((block_rows, tile_cols), jnp.int32)
    tile_row = (row_first + jnp.arange(block_rows, dtype=jnp.int32)[:, None] + zero_grid).reshape(
        tile_count, 1
    )
    tile_start = (TILE_COLS * jnp.arange(tile_cols, dtype=jnp.int32)[None, :]).reshape(
        tile_count, 1
    )
    row_gap = (obs_row - tile_row).astype(jnp.float32)
    col_twice = 2 * obs_col - 2 * tile_start - (TILE_COLS - 1)
    col_twice = (col_twice + grid_cols) % (2 * grid_cols) - grid_cols
    col_gap = 0.5 * col_twice.astype(jnp.float32)
    distance = row_gap * row_gap + col_gap * col_gap
    tapering = jnp.exp(-distance / (2.0 * LOC_RADIUS * LOC_RADIUS))
    sigma_sel = jnp.take(obs_sigma, global_flat)
    obs_weight = tapering / (sigma_sel * sigma_sel)
    innovation = jnp.take(obs_value, global_flat) - chosen_mean
    weighted = chosen * obs_weight[None]
    gram_matrix = jnp.einsum("knl,jnl->nkj", weighted, chosen, precision=highest)
    identity = jnp.eye(members, dtype=jnp.float32)
    system = gram_matrix + (members - 1.0) * identity
    frob_norm = jnp.sqrt(jnp.sum(system * system, axis=(1, 2)))
    iterate = system / frob_norm[:, None, None]
    inverse_root = jnp.broadcast_to(identity, system.shape)
    for sweep_index in range(NS_ITERS):
        factor = 1.5 * identity - 0.5 * jnp.einsum(
            "nij,njk->nik", inverse_root, iterate, precision=highest
        )
        iterate = jnp.einsum("nij,njk->nik", iterate, factor, precision=highest)
        inverse_root = jnp.einsum("nij,njk->nik", factor, inverse_root, precision=highest)
    forcing = jnp.einsum("knl,nl->nk", chosen, obs_weight * innovation, precision=highest)
    half_step = jnp.einsum("nkj,nj->nk", inverse_root, forcing, precision=highest)
    mean_weight = (
        jnp.einsum("nkj,nj->nk", inverse_root, half_step, precision=highest) / frob_norm[:, None]
    )
    transform = (
        jnp.sqrt(members - 1.0) * inverse_root / jnp.sqrt(frob_norm)[:, None, None]
        + mean_weight[:, :, None]
    )
    tile_cells = ensemble_block.reshape(members, tile_count, TILE_COLS)
    centre_mean = jnp.mean(tile_cells, axis=0)
    spread = tile_cells - centre_mean
    analysis = centre_mean + jnp.einsum("jnt,njk->knt", spread, transform, precision=highest)
    return analysis.reshape(members, block_rows, block_cols)


def on_device(
    ensemble,
    spreading_number,
    zonal_transport_ratio,
    meridional_transport_ratio,
    ocean_mask,
    obs_loc,
    obs_value,
    obs_sigma,
    tile_obs,
):
    mem_dev, row_count, col_count = ensemble.shape
    liquid_cell_flags = ocean_mask.astype(jnp.float32)
    level_state_grid = liquid_cell_flags * ensemble
    for prior_step_tally in range(2):
        haloed_state_grid = padded(level_state_grid, (("space", 1),), 1)
        level_state_grid = propagate_prior_state(
            haloed_state_grid,
            spreading_number,
            zonal_transport_ratio,
            meridional_transport_ratio,
            liquid_cell_flags,
        )
    space_index = lax.axis_index("space")
    member_index = lax.axis_index("member")
    obs_dev = obs_loc.shape[0] // lax.axis_size("space")
    flattened = level_state_grid.reshape(mem_dev, row_count * col_count)
    own_loc = lax.dynamic_slice_in_dim(obs_loc, space_index * obs_dev, obs_dev) - space_index * (
        row_count * col_count
    )
    own_obs = jnp.take(flattened, own_loc, axis=1)
    rimmed = padded(own_obs, (("space", 1),), obs_dev)
    window = lax.all_gather(rimmed, "member", axis=0, tiled=True)
    window_mean = jnp.mean(window, axis=0)
    window_anom = window - window_mean
    first_obs = (space_index - 1) * obs_dev
    cell_block = lax.all_to_all(level_state_grid, "member", split_axis=1, concat_axis=0, tiled=True)
    block_rows = cell_block.shape[1]
    tile_picks = lax.dynamic_slice_in_dim(tile_obs, member_index * block_rows, block_rows, 0)
    row_first = space_index * row_count + member_index * block_rows
    updated = analyze(
        cell_block,
        window_anom,
        window_mean,
        tile_picks - first_obs,
        tile_picks,
        obs_loc,
        obs_value,
        obs_sigma,
        row_first,
        col_count,
    )
    result = lax.all_to_all(updated, "member", split_axis=0, concat_axis=1, tiled=True)
    return result


def solution(mesh):
    in_specs = (
        P("member", "space", None),
        P("space", None),
        P("space", None),
        P("space", None),
        P("space", None),
        P(),
        P(),
        P(),
        P("space", None, None),
    )
    out_specs = P("member", "space", None)
    return jax.shard_map(
        on_device, mesh=mesh, in_specs=in_specs, out_specs=out_specs, check_vma=False
    )
```

profile of v0, /device:TPU:135, one launch (start us, length us, event | category | flops | bytes accessed | tf_op | source)
XLA Modules:
  0.0 264.1 jit_solution(4438026038284993184)
XLA Ops:
  6.6 1.0 convert_element_type.14
  7.6 1.5 copy_multiply_fusion
  9.1 2.6 collective-permute-start
  11.6 7.2 %collective-permute-start.1 = (f32[4,1,2048]{2,0,1:T(4,128)S(1)}, f32[4,1,2048]{2,0,1:T(4,128)S(1)}, u32[]{:S(2)}, u32[]{:S(2)}) collective-permute-start(f32[4,1,2048]{2,0,1:T(4,128)S(1)} %get-tuple-element.15), channel_id=1, source_target_pairs={{0,1},{1,2},{2,3},{3,4},{4,5},{5,6},{6,7},{7,8},{8,9},{9,10},{10,1... | collective-permute-start | bytes 98312 | tf_op jit(solution)/shard_map/ppermute | solution.py:22
  18.8 0.3 fusion.68
  19.3 0.5 collective-permute-done.1
  19.9 0.7 subtract_multiply_fusion.1
  20.6 0.3 fusion.65
  20.9 1.9 collective-permute-start.2
  22.9 8.4 %collective-permute-start.3 = (f32[4,1,2048]{2,0,1:T(4,128)S(1)}, f32[4,1,2048]{2,0,1:T(4,128)S(1)}, u32[]{:S(2)}, u32[]{:S(2)}) collective-permute-start(f32[4,1,2048]{2,0,1:T(4,128)S(1)} %get-tuple-element.9), channel_id=1, source_target_pairs={{0,1},{1,2},{2,3},{3,4},{4,5},{5,6},{6,7},{7,8},{8,9},{9,10},{10,1... | collective-permute-start | bytes 98312 | tf_op jit(solution)/shard_map/ppermute | solution.py:22
  31.4 0.9 collective-permute-done.3
  32.3 1.5 subtract_multiply_fusion
  33.9 9.7 %copy.35 = f32[4,16,2048]{0,2,1:T(8,128)} copy(f32[4,16,2048]{2,0,1:T(4,128)} %subtract_multiply_fusion) | data formatting | bytes 1048576 | tf_op jit(solution)/shard_map/mul | solution.py:48
  43.6 11.2 %gather_fusion = f32[2048,4]{1,0:T(8,128)S(1)} fusion(f32[4,32768]{0,1:T(8,128)} %bitcast.111, s32[2048]{0:T(1024)S(1)} %fusion.59), kind=kCustom, calls=%fused_computation.2 | custom fusion | bytes 73728 | tf_op jit(solution)/shard_map/jit(_take)/gather | solution.py:148
  54.8 0.3 select_bitcast_fusion
  55.2 0.3 copy.36
  55.5 8.4 %collective-permute-start.4 = (f32[4,2048]{1,0:T(4,128)S(1)}, f32[4,2048]{1,0:T(4,128)S(1)}, u32[]{:S(2)}, u32[]{:S(2)}) collective-permute-start(f32[4,2048]{1,0:T(4,128)S(1)} %copy.36), channel_id=1, source_target_pairs={{0,1},{1,2},{2,3},{3,4},{4,5},{5,6},{6,7},{7,8},{8,9},{9,10},{10,1... | collective-permute-start | bytes 98312 | tf_op jit(solution)/shard_map/ppermute | solution.py:22
  63.9 1.9 collective-permute-start.5
  65.9 7.5 %collective-permute-done.5 = f32[4,2048]{1,0:T(4,128)S(1)} collective-permute-done((f32[4,2048]{1,0:T(4,128)S(1)}, f32[4,2048]{1,0:T(4,128)S(1)}, u32[]{:S(2)}, u32[]{:S(2)}) %collective-permute-start.5) | collective-permute-done | bytes 32800 | tf_op jit(solution)/shard_map/ppermute | solution.py:24
  73.4 0.7 maximum_bitcast_fusion
  74.1 0.7 fusion.52
  74.9 23.0 %gather_fusion.2 = s32[4096]{0:T(1024)S(1)} fusion(s32[65536]{0:T(1024)S(1)} %copy-done.1, s32[4096]{0:T(1024)S(1)} %broadcast_clamp_fusion.1), kind=kCustom, calls=%fused_computation.4 | custom fusion | bytes 49152 | tf_op jit(solution)/shard_map/jit(_take)/gather | solution.py:70
  97.9 0.6 reshape.192
  98.5 8.8 %all-to-all-start = ((f32[4,16,2048]{2,0,1:T(4,128)}), f32[4,16,2048]{2,0,1:T(4,128)S(1)}, u32[]{:S(2)}, u32[]{:S(2)}) async-start(f32[4,16,2048]{2,0,1:T(4,128)} %subtract_multiply_fusion), calls=%async_computation | async-start | bytes 1048576 | tf_op jit(solution)/shard_map/all_to_all | solution.py:154
  107.3 0.7 fusion.58
  108.1 23.0 %gather_fusion.4 = f32[4096]{0:T(1024)S(1)} fusion(f32[65536]{0:T(1024)S(1)} %copy-done, s32[4096]{0:T(1024)S(1)} %broadcast_clamp_fusion), kind=kCustom, calls=%fused_computation.clone | custom fusion | bytes 49152 | tf_op jit(solution)/shard_map/jit(_take)/gather | solution.py:86
  131.1 0.6 reshape.220
  131.7 23.0 %gather_fusion.5 = f32[4096]{0:T(1024)S(1)} fusion(f32[65536]{0:T(1024)S(1)} %copy-done.2, s32[4096]{0:T(1024)S(1)} %broadcast_clamp_fusion), kind=kCustom, calls=%fused_computation.1.clone | custom fusion | bytes 49152 | tf_op jit(solution)/shard_map/jit(_take)/gather | solution.py:88
  154.7 0.6 reshape.224
  155.4 0.5 iota_multiply_fusion
  156.3 0.8 broadcast_subtract_fusion.1
  157.1 1.8 reduce_sum.28
  159.0 0.5 reshape.216
  159.6 1.3 broadcast_subtract_fusion
  160.8 2.1 copy.39
  162.9 40.5 %gather_fusion.3 = f32[4096]{0:T(1024)} fusion(f32[6144]{0:T(1024)S(1)} %broadcast_multiply_fusion, s32[4096]{0:T(1024)S(1)} %broadcast_clamp_fusion.2), kind=kCustom, calls=%fused_computation.5 | custom fusion | bytes 49152 | tf_op jit(solution)/shard_map/jit(_take)/gather | solution.py:69
  203.4 14.1 %gather_fusion.1 = f32[4096,64]{1,0:T(8,128)} fusion(f32[64,6144]{0,1:T(8,128)S(1)} %copy.39, s32[4096]{0:T(1024)S(1)} %broadcast_clamp_fusion.2), kind=kCustom, calls=%fused_computation.3 | custom fusion | bytes 2113536 | tf_op jit(solution)/shard_map/jit(_take)/gather | solution.py:68
  217.6 2.2 copy.40
  219.8 0.8 fusion.55
  220.7 1.3 multiply_reduce_fusion
  222.0 0.7 fusion.11
  222.6 0.7 fusion.31
  223.4 0.6 fusion.28
  223.9 0.6 fusion.10
  224.6 0.6 fusion.71
  225.2 0.6 fusion.70
  225.9 0.6 fusion.9
  226.5 0.6 fusion.73
  227.2 0.6 fusion.72
  227.8 0.6 fusion.8
  228.5 0.6 fusion.75
  229.1 0.6 fusion.74
  229.8 0.6 fusion.7
  230.5 0.6 fusion.77
  231.1 0.6 fusion.76
  231.8 1.3 convolution_bitcast_fusion
  233.0 0.7 fusion.6
  233.7 0.6 fusion.78
  234.3 0.9 convolution_bitcast_fusion.1
  235.2 0.9 fusion.79
  236.3 1.3 fusion.5
  237.5 0.3 copy.43
  237.9 18.3 %all_to_all.33 = f32[64,1,2048]{2,1,0:T(1,128)S(1)} all-to-all(f32[64,1,2048]{2,1,0:T(1,128)S(1)} %bitcast.114), channel_id=1, replica_groups=mesh['member'=16,'space'=32] {'member'}, dimensions={0} | all-to-all | bytes 1048576 | tf_op jit(solution)/shard_map/all_to_all | solution.py:170
  256.1 1.1 copy.63
  (55 shorter events, 0.9 us)
Async XLA Ops:
  6.5 101.5 %copy-start = (f32[65536]{0:T(1024)S(1)}, f32[65536]{0:T(1024)}, u32[]{:S(2)}) copy-start(f32[65536]{0:T(1024)} %param.18) | copy-start | bytes 786436
  6.5 12.7 %copy-start.1 = (s32[65536]{0:T(1024)S(1)}, s32[65536]{0:T(1024)}, u32[]{:S(2)}) copy-start(s32[65536]{0:T(1024)} %param.16) | copy-start | bytes 786436
  6.5 13.3 %copy-start.7 = (f32[16,2048]{1,0:T(8,128)S(1)}, f32[16,2048]{1,0:T(8,128)}, u32[]{:S(2)}) copy-start(f32[16,2048]{1,0:T(8,128)} %param.12) | copy-start | bytes 393220
  6.5 13.3 %copy-start.6 = (f32[16,2048]{1,0:T(8,128)S(1)}, f32[16,2048]{1,0:T(8,128)}, u32[]{:S(2)}) copy-start(f32[16,2048]{1,0:T(8,128)} %param.13) | copy-start | bytes 393220
  6.5 13.3 %copy-start.5 = (f32[16,2048]{1,0:T(8,128)S(1)}, f32[16,2048]{1,0:T(8,128)}, u32[]{:S(2)}) copy-start(f32[16,2048]{1,0:T(8,128)} %param.14) | copy-start | bytes 393220
  6.5 150.6 %all-gather.3.cloned.1.call-start = ((), (), s32[]{:S(2)}) async-start(), calls=%async_computation.2 | async-start | bytes 1671168 | tf_op jit(solution)/shard_map/all_gather | solution.py:150
  9.1 10.3 %collective-permute-start = (f32[4,1,2048]{2,0,1:T(4,128)S(1)}, f32[4,1,2048]{2,0,1:T(4,128)S(1)}, u32[]{:S(2)}, u32[]{:S(2)}) collective-permute-start(f32[4,1,2048]{2,0,1:T(4,128)S(1)} %get-tuple-element.16), channel_id=1, source_target_pairs={{1,0},{2,1},{3,2},{4,3},{5,4},{6,5},{7,6},{8,7},{9,8},{10,9},{11,1... | collective-permute-start | bytes 98312 | tf_op jit(solution)/shard_map/ppermute | solution.py:24
  11.6 8.2 %collective-permute-start.1 = (f32[4,1,2048]{2,0,1:T(4,128)S(1)}, f32[4,1,2048]{2,0,1:T(4,128)S(1)}, u32[]{:S(2)}, u32[]{:S(2)}) collective-permute-start(f32[4,1,2048]{2,0,1:T(4,128)S(1)} %get-tuple-element.15), channel_id=1, source_target_pairs={{0,1},{1,2},{2,3},{3,4},{4,5},{5,6},{6,7},{7,8},{8,9},{9,10},{10,1... | collective-permute-start | bytes 98312 | tf_op jit(solution)/shard_map/ppermute | solution.py:22
  20.9 10.5 %collective-permute-start.2 = (f32[4,1,2048]{2,0,1:T(4,128)S(1)}, f32[4,1,2048]{2,0,1:T(4,128)S(1)}, u32[]{:S(2)}, u32[]{:S(2)}) collective-permute-start(f32[4,1,2048]{2,0,1:T(4,128)S(1)} %get-tuple-element.10), channel_id=1, source_target_pairs={{1,0},{2,1},{3,2},{4,3},{5,4},{6,5},{7,6},{8,7},{9,8},{10,9},{11,1... | collective-permute-start | bytes 98312 | tf_op jit(solution)/shard_map/ppermute | solution.py:24
  22.9 9.5 %collective-permute-start.3 = (f32[4,1,2048]{2,0,1:T(4,128)S(1)}, f32[4,1,2048]{2,0,1:T(4,128)S(1)}, u32[]{:S(2)}, u32[]{:S(2)}) collective-permute-start(f32[4,1,2048]{2,0,1:T(4,128)S(1)} %get-tuple-element.9), channel_id=1, source_target_pairs={{0,1},{1,2},{2,3},{3,4},{4,5},{5,6},{6,7},{7,8},{8,9},{9,10},{10,1... | collective-permute-start | bytes 98312 | tf_op jit(solution)/shard_map/ppermute | solution.py:22
  55.5 10.4 %collective-permute-start.4 = (f32[4,2048]{1,0:T(4,128)S(1)}, f32[4,2048]{1,0:T(4,128)S(1)}, u32[]{:S(2)}, u32[]{:S(2)}) collective-permute-start(f32[4,2048]{1,0:T(4,128)S(1)} %copy.36), channel_id=1, source_target_pairs={{0,1},{1,2},{2,3},{3,4},{4,5},{5,6},{6,7},{7,8},{8,9},{9,10},{10,1... | collective-permute-start | bytes 98312 | tf_op jit(solution)/shard_map/ppermute | solution.py:22
  63.9 9.5 %collective-permute-start.5 = (f32[4,2048]{1,0:T(4,128)S(1)}, f32[4,2048]{1,0:T(4,128)S(1)}, u32[]{:S(2)}, u32[]{:S(2)}) collective-permute-start(f32[4,2048]{1,0:T(4,128)S(1)} %copy.36), channel_id=1, source_target_pairs={{1,0},{2,1},{3,2},{4,3},{5,4},{6,5},{7,6},{8,7},{9,8},{10,9},{11,1... | collective-permute-start | bytes 98312 | tf_op jit(solution)/shard_map/ppermute | solution.py:24
  98.5 57.4 %all-to-all-start = ((f32[4,16,2048]{2,0,1:T(4,128)}), f32[4,16,2048]{2,0,1:T(4,128)S(1)}, u32[]{:S(2)}, u32[]{:S(2)}) async-start(f32[4,16,2048]{2,0,1:T(4,128)} %subtract_multiply_fusion), calls=%async_computation | async-start | bytes 1048576 | tf_op jit(solution)/shard_map/all_to_all | solution.py:154
  108.1 23.7 %copy-start.2 = (f32[65536]{0:T(1024)S(1)}, f32[65536]{0:T(1024)}, u32[]{:S(2)}) copy-start(f32[65536]{0:T(1024)} %param.17) | copy-start | bytes 786436
  157.1 1.9 copy-start.3
  217.5 2.2 copy-start.11
  217.5 2.3 copy-start.8
  217.5 2.3 copy-start.9
  217.5 2.3 copy-start.10
  217.5 2.3 copy-start.12
  233.0 3.3 %copy-start.4 = (f32[64,16,128]{2,1,0:T(8,128)S(1)}, f32[64,16,128]{2,1,0:T(8,128)}, u32[]{:S(2)}) copy-start(f32[64,16,128]{2,1,0:T(8,128)} %broadcast_subtract_fusion.1) | copy-start | bytes 1572868
Sparse Core Ops, SparseCore 0:
  74.2 66.8 all-gather.2
where the time goes:
time: 265 us; the launch traced here: 264 us
  local copies, waits for them, and re-layouts  154 us (58%)
  starting transfers between devices  39.3 us (15%)
  blocking collectives  18.3 us (7%)
  matrix products  16.6 us (6%)
  between operations  13.9 us (5%)
  other arithmetic  12.6 us (5%)
  waiting for transfers between devices  8.96 us (3%)
    gather x2, local copies, waits for them, and re-layouts, analyze(): chosen_mean = jnp.take(means, window_flat)  40.5 us
    ppermute x3, starting transfers between devices, padded(): lax.ppermute(tail, axis, [(i, (i + 1) % count) for i in range(ends)])  24.1 us
    gather x2, local copies, waits for them, and re-layouts, analyze(): location = jnp.take(obs_loc, global_flat)  23.6 us
    gather x2, local copies, waits for them, and re-layouts, analyze(): sigma_sel = jnp.take(obs_sigma, global_flat)  23.6 us
    gather x2, local copies, waits for them, and re-layouts, analyze(): innovation = jnp.take(obs_value, global_flat) - chosen_mean  23.6 us
    all_to_all x1, blocking collectives, on_device(): lax.all_to_all(updated, 'member', split_axis=0, concat_axis=1, tiled=True)  18.3 us
    gather x2, local copies, waits for them, and re-layouts, analyze(): chosen = jnp.take(anomalies, window_flat, axis=1)  16.3 us
    gather x1, local copies, waits for them, and re-layouts, on_device(): own_obs = jnp.take(flattened, own_loc, axis=1)  11.2 us
  transfers between devices with their start and end apart: 8, of which 3 were waited for; matrix products, arithmetic and copies ran while one was open for 28% of the time, Pallas kernels for 0%

commit v1 on v0

v1 whole, which is shorter than its diff:
```python
import functools

import jax
import jax.numpy as jnp
from jax import lax
from jax.experimental import pallas as pl
from jax.experimental.pallas import tpu as pltpu
from jax.sharding import PartitionSpec as P

LOC_RADIUS = 96
MESH = pl.DeviceIdType.MESH
f32 = jnp.float32
bf16 = jnp.bfloat16
i32 = jnp.int32
MEM = 16
NYD = 8
SPACE = 32
KM = 4
ROWS = 16
COLS = 2048
OBS = 2048


def split(x):
    hi = x.astype(bf16)
    return hi, (x - hi.astype(f32)).astype(bf16)


def mm(a, b):
    return jnp.dot(a, b, preferred_element_type=f32)


def mm3(a, b):
    ah, al = split(a)
    bh, bl = split(b)
    return mm(ah, bh) + (mm(al, bh) + mm(ah, bl))


def forecast(ens, spr, zon, mer, mask, hu_lo, hc_lo, hu_hi, hc_hi, field, first, last):
    s, z, m = spr[...], zon[...] * 0.5, mer[...] * 0.5
    sea = mask[...].astype(f32)

    def step(centre, north, south, s, z, m, sea):
        east = pltpu.roll(centre, COLS - 1, 1)
        west = pltpu.roll(centre, 1, 1)
        lap = north + south + east + west - 4.0 * centre
        adv = z * (east - west) + m * (north - south)
        return sea * (centre + s * lap - adv)

    lo = jnp.where(first, 0.0, hu_lo[...])
    hi = jnp.where(last, 0.0, hu_hi[...])
    south2, south1 = lo[0:KM], lo[KM:]
    north1, north2 = hi[0:KM], hi[KM:]
    own_first = jnp.concatenate([sea[0:1] * ens[k, 0:1] for k in range(KM)], axis=0)
    own_last = jnp.concatenate([sea[ROWS - 1 :] * ens[k, ROWS - 1 :] for k in range(KM)], axis=0)

    def coef(ref, edge):
        c = ref[...]
        return c[0:1], c[1:2] * 0.5, c[2:3] * 0.5, jnp.where(edge, 0.0, c[3:4])

    below = step(south1, own_first, south2, *coef(hc_lo, first))
    above = step(north1, north2, own_last, *coef(hc_hi, last))
    for k in range(KM):
        u = sea * ens[k]
        north = jnp.concatenate([u[1:], north1[k : k + 1]], axis=0)
        south = jnp.concatenate([south1[k : k + 1], u[: ROWS - 1]], axis=0)
        u = step(u, north, south, s, z, m, sea)
        north = jnp.concatenate([u[1:], above[k : k + 1]], axis=0)
        south = jnp.concatenate([below[k : k + 1], u[: ROWS - 1]], axis=0)
        field[k] = step(u, north, south, s, z, m, sea)


def observe(field, loc, hx):
    sub = lax.broadcasted_iota(i32, (8, 128), 0)

    def body(g, _):
        at = loc[1, pl.ds(g, 1), :]
        row = jnp.broadcast_to((at >> 11) & (ROWS - 1), (8, 128))
        blk = jnp.broadcast_to((at >> 7) & 15, (8, 128))
        lane = jnp.broadcast_to(at & 127, (8, 128))
        acc = [jnp.zeros((8, 128), f32) for _ in range(2 * KM)]
        for b in range(16):
            hit = blk == b
            for k in range(KM):
                for h in range(2):
                    v = field[k, 8 * h : 8 * h + 8, 128 * b : 128 * b + 128]
                    got = jnp.take_along_axis(v, lane, axis=1, mode="promise_in_bounds")
                    acc[2 * k + h] = jnp.where(hit, got, acc[2 * k + h])
        for k in range(KM):
            mine = jnp.where(row == sub, acc[2 * k], 0.0) + jnp.where(
                row == sub + 8, acc[2 * k + 1], 0.0
            )
            hx[g & 7, pl.ds((g >> 3) * KM + k, 1), :] = jnp.sum(mine, axis=0, keepdims=True)
        return 0

    lax.fori_loop(0, 16, body, 0)


def weigh(lo, hi, picks, loc, val, sig, rinv, vals, row0, mid2):
    sub = lax.broadcasted_iota(i32, (8, 128), 0)

    def body(p, _):
        ix = picks[pl.ds(p, 1), :]
        blk = jnp.broadcast_to(ix >> 7, (8, 128))
        lane = jnp.broadcast_to(ix & 127, (8, 128))
        acc = [jnp.zeros((8, 128), i32), jnp.zeros((8, 128), f32), jnp.zeros((8, 128), f32)]
        for v in range(6):
            hit = (blk - 8 * v) == sub
            for q, ref in enumerate((loc, val, sig)):
                got = jnp.take_along_axis(
                    ref[v // 2, 8 * (v % 2) : 8 * (v % 2) + 8, :],
                    lane,
                    axis=1,
                    mode="promise_in_bounds",
                )
                acc[q] = jnp.where(hit, got, acc[q])
        at, value, sigma = [jnp.sum(a, axis=0, keepdims=True) for a in acc]
        row_gap = ((at >> 11) - (row0 + (p >> 1))).astype(f32)
        twice = 2 * (at & (COLS - 1)) - mid2
        twice = ((twice + COLS) & (2 * COLS - 1)) - COLS
        col_gap = 0.5 * twice.astype(f32)
        distance = row_gap * row_gap + col_gap * col_gap
        taper = jnp.exp(-distance / (2.0 * LOC_RADIUS * LOC_RADIUS))
        rinv[pl.ds(p, 1), :] = taper / (sigma * sigma)
        vals[pl.ds(p, 1), :] = value
        return 0

    lax.fori_loop(lo, hi, body, 0)


def tabulate(band, win, table):
    def body(cb, _):
        vs = [win[band, m, cb] for m in range(MEM)]
        for half in range(2):
            x = jnp.concatenate([v[KM * half : KM * half + KM] for v in vs], axis=0)
            mean = jnp.sum(x, axis=0, keepdims=True) * (1.0 / 64)
            full = jnp.concatenate([x - mean, jnp.broadcast_to(mean, (64, 128))], axis=0)
            at = band * OBS + half * 1024 + cb * 128
            table[pl.ds(pl.multiple_of(at, 128), 128), :] = full.T
        return 0

    lax.fori_loop(0, 8, body, 0)


def fetch(t, idx, table, chosen, unroll=32):
    def body(j, _):
        rows = []
        for u in range(unroll):
            i = j * unroll + u
            rows.append(table[pl.ds(idx[2 * t + (i >> 7), i & 127], 1), :])
        for u in range(unroll):
            chosen[pl.ds(j * unroll + u, 1), :] = rows[u]
        return 0

    lax.fori_loop(0, 256 // unroll, body, 0)


def gram(t, chosen, rinv, vals, start, force, scale):
    a = chosen[...]
    at = a.T
    r = jnp.concatenate([rinv[pl.ds(2 * t, 1), :], rinv[pl.ds(2 * t + 1, 1), :]], axis=1)
    v = jnp.concatenate([vals[pl.ds(2 * t, 1), :], vals[pl.ds(2 * t + 1, 1), :]], axis=1)
    w = jnp.concatenate(
        [at[0:64] * r, jnp.broadcast_to(r * (v - at[64:65]), (8, 256))], axis=0
    )
    g = mm3(w, a)
    ii = lax.broadcasted_iota(i32, (64, 128), 0)
    jj = lax.broadcasted_iota(i32, (64, 128), 1)
    system = jnp.where(jj < 64, g[0:64], 0.0) + jnp.where(ii == jj, 63.0, 0.0)
    square = jnp.sum(jnp.sum(system * system, axis=0, keepdims=True), axis=1, keepdims=True)
    inv = lax.rsqrt(square)
    start[t] = system * inv
    force[pl.ds(t, 1), :] = g[64:65]
    scale[pl.ds(t, 1), :] = jnp.broadcast_to(inv, (1, 128))


def pack(start, t):
    def pair(a, b):
        lane = lax.broadcasted_iota(i32, a.shape, 1)
        return jnp.where(lane < 64, a, pltpu.roll(b, 64, 1))

    return jnp.concatenate(
        [pair(start[t], start[t + 1]), pair(start[t + 2], start[t + 3])], axis=1
    )


def diagonal(x):
    quarter = lax.broadcasted_iota(i32, x.shape, 1) >> 6
    return jnp.concatenate(
        [jnp.where(quarter == i, x, jnp.zeros_like(x)) for i in range(4)], axis=0
    ).astype(bf16)


def newton(xs):
    ii = lax.broadcasted_iota(i32, (64, 256), 0)
    jj = lax.broadcasted_iota(i32, (64, 256), 1) & 63
    eye = jnp.where(ii == jj, 1.5, 0.0).astype(f32)
    zs = None

    def dot(left, right):
        h, l = split(left)
        return mm(h, right[0]) + (mm(l, right[0]) + mm(h, right[1]))

    for it in range(6):
        fs = [eye - 0.5 * x for x in xs]
        blocks = []
        for f in fs:
            h, l = split(f)
            blocks.append((diagonal(h.astype(f32)), diagonal(l.astype(f32))))
        if it == 0:
            ps = [dot(x, b) for x, b in zip(xs, blocks)]
            zs = fs
            xs = [dot(p, b) for p, b in zip(ps, blocks)]
        elif it < 5:
            both = [
                dot(jnp.concatenate([x, z], axis=0), b) for x, z, b in zip(xs, zs, blocks)
            ]
            zs = [q[64:] for q in both]
            xs = [dot(q[:64], b) for q, b in zip(both, blocks)]
        else:
            zs = [dot(z, b) for z, b in zip(zs, blocks)]
    return zs


def transform_pair(t, z, force, scale, cells, out):
    lane = lax.broadcasted_iota(i32, (64, 128), 1)
    lane1 = lane[0:1]
    g = jnp.where(lane1 < 64, force[pl.ds(t, 1), :], pltpu.roll(force[pl.ds(t + 1, 1), :], 64, 1))
    inv = jnp.where(lane1 < 64, scale[pl.ds(t, 1), :], scale[pl.ds(t + 1, 1), :])
    q = z * g
    h0 = jnp.sum(jnp.where(lane < 64, q, 0.0), axis=1, keepdims=True)
    h1 = jnp.sum(jnp.where(lane < 64, 0.0, q), axis=1, keepdims=True)
    wbar = jnp.sum(z * jnp.where(lane < 64, h0, h1), axis=0, keepdims=True) * inv
    weights = jnp.sqrt(63.0 * inv) * z + wbar
    xs, means = [], []
    for i in range(2):
        x = cells[pl.ds(t + i, 64, stride=ROWS), :]
        mean = jnp.sum(x, axis=0, keepdims=True) * (1.0 / 64)
        xs.append(x - mean)
        means.append(mean)
    none = jnp.zeros((64, 128), f32)
    block = jnp.concatenate(
        [jnp.concatenate([xs[0], none], axis=1), jnp.concatenate([none, xs[1]], axis=1)], axis=0
    )
    moved = mm3(weights, block)
    for i in range(2):
        out[pl.ds(t + i, 64, stride=ROWS), :] = means[i] + moved[:, 128 * i : 128 * i + 128]


PARTS = 2


def kernel(
    ens_h, spr_h, zon_h, mer_h, mask_h, loc_h, val_h, sig_h, tile_h, out,
    ens, spr, zon, mer, mask, loc, val, sig, tile, picks, idx,
    send_u, send_c, hu_lo, hc_lo, hu_hi, hc_hi, field, hx, win, rinv, vals, table, chosen,
    start, force, scale, cells, done,
    load_sem, obs_sem, halo_send, halo_recv, y_send, y_recv, z_send, z_recv,
    lo_send, lo_recv, hi_send, hi_recv, c_send, c_recv, a_send, a_recv, local_sem,
):
    me = lax.axis_index("member")
    sp = lax.axis_index("space")
    zz, yy = me // NYD, me % NYD
    below, above = (sp + SPACE - 1) % SPACE, (sp + 1) % SPACE
    other = me ^ NYD

    loads = [
        pltpu.make_async_copy(a, b, load_sem.at[i])
        for i, (a, b) in enumerate(
            [(ens_h, ens), (mask_h, mask), (spr_h, spr), (zon_h, zon), (mer_h, mer), (tile_h, tile)]
        )
    ]
    for j in range(3):
        band = jnp.clip(sp - 1 + j, 0, SPACE - 1)
        for i, (a, b) in enumerate([(loc_h, loc), (val_h, val), (sig_h, sig)]):
            loads.append(pltpu.make_async_copy(a.at[band], b.at[j], obs_sem.at[3 * j + i]))
    for copy in loads:
        copy.start()

    barrier = pltpu.get_barrier_semaphore()
    for i in range(1, MEM):
        pl.semaphore_signal(barrier, inc=1, device_id=((me + i) % MEM, sp), device_id_type=MESH)
    for to in (below, above):
        pl.semaphore_signal(barrier, inc=1, device_id=(me, to), device_id_type=MESH)
    for copy in loads[:5]:
        copy.wait()

    for side, (r1, r2, edge) in enumerate([(0, 1, 0), (ROWS - 2, ROWS - 1, ROWS - 1)]):
        for j, r in enumerate((r1, r2)):
            sea = mask[r : r + 1, :].astype(f32)
            for k in range(KM):
                send_u[side, j * KM + k : j * KM + k + 1, :] = sea * ens[k, r : r + 1, :]
        for q, ref in enumerate((spr, zon, mer)):
            send_c[side, q : q + 1, :] = ref[edge : edge + 1, :]
        send_c[side, 3:4, :] = mask[edge : edge + 1, :].astype(f32)
    pl.semaphore_wait(barrier, MEM + 1)

    def remote(src, dst, send, recv, to):
        return pltpu.make_async_remote_copy(
            src_ref=src, dst_ref=dst, send_sem=send, recv_sem=recv, device_id=to, device_id_type=MESH
        )

    halos = [
        remote(send_u.at[0], hu_hi, halo_send.at[0], halo_recv.at[0], (me, below)),
        remote(send_c.at[0], hc_hi, halo_send.at[1], halo_recv.at[1], (me, below)),
        remote(send_u.at[1], hu_lo, halo_send.at[2], halo_recv.at[2], (me, above)),
        remote(send_c.at[1], hc_lo, halo_send.at[3], halo_recv.at[3], (me, above)),
    ]
    for copy in halos:
        copy.start()
    for copy in loads[5:]:
        copy.wait()
    first_obs = (sp - 1) * OBS
    for r in range(ROWS):
        row = jnp.clip(tile[r, pl.ds(me, 1), :] - first_obs, 0, 3 * OBS - 1)
        picks[2 * r : 2 * r + 1, :] = row[:, 0:128]
        picks[2 * r + 1 : 2 * r + 2, :] = row[:, 128:256]
    to_scalar = pltpu.make_async_copy(picks, idx, local_sem.at[0])
    to_scalar.start()
    for copy in halos:
        copy.wait()

    forecast(ens, spr, zon, mer, mask, hu_lo, hc_lo, hu_hi, hc_hi, field, sp == 0, sp == SPACE - 1)
    observe(field, loc, hx)

    def to_lo(src, slot, i):
        return remote(src, win.at[2, slot], lo_send.at[i], lo_recv.at[i], (me, below))

    def to_hi(src, slot, i):
        return remote(src, win.at[0, slot], hi_send.at[i], hi_recv.at[i], (me, above))

    def to_z(src, slot, i):
        return remote(src, win.at[1, slot], z_send.at[i], z_recv.at[i], (other, sp))

    keep = pltpu.make_async_copy(hx, win.at[1, me], local_sem.at[1])
    keep.start()
    steps = (1, 7, 2, 6, 3, 5, 4)
    ys = [
        remote(hx, win.at[1, me], y_send.at[i], y_recv.at[i], (zz * NYD + (yy + d) % NYD, sp))
        for i, d in enumerate(steps)
    ]
    zs, los, his = [to_z(hx, me, 0)], [to_lo(hx, me, 0)], [to_hi(hx, me, 0)]
    for copy in ys + zs + los + his:
        copy.start()
    row0, mid2 = sp * ROWS, 2 * 128 * me + 127

    def some(i):
        weigh(2 * i, 2 * i + 2, picks, loc, val, sig, rinv, vals, row0, mid2)

    for i, d in enumerate(steps):
        some(i)
        ys[i].wait_recv()
        slot = zz * NYD + (yy + NYD - d) % NYD
        src = win.at[1, slot]
        zs.append(to_z(src, slot, i + 1))
        los.append(to_lo(src, slot, i + 1))
        his.append(to_hi(src, slot, i + 1))
        for copy in (zs[-1], los[-1], his[-1]):
            copy.start()
    for i, d in enumerate((0,) + steps):
        some(7 + i)
        zs[i].wait_recv()
        slot = (1 - zz) * NYD + (yy + NYD - d) % NYD
        src = win.at[1, slot]
        los.append(to_lo(src, slot, i + 8))
        his.append(to_hi(src, slot, i + 8))
        for copy in (los[-1], his[-1]):
            copy.start()
    some(15)

    cs = []
    for i in range(1, MEM):
        to = (me + i) % MEM
        cs.append(
            remote(
                field.at[:, :, pl.ds(pl.multiple_of(128 * to, 128), 128)],
                cells.at[pl.ds(KM * me, KM)],
                c_send.at[i],
                c_recv.at[i],
                (to, sp),
            )
        )
        cs[-1].start()
    own = pltpu.make_async_copy(
        field.at[:, :, pl.ds(pl.multiple_of(128 * me, 128), 128)],
        cells.at[pl.ds(KM * me, KM)],
        local_sem.at[2],
    )
    own.start()

    keep.wait()
    tabulate(1, win, table)
    for copy in his:
        copy.wait_recv()
    tabulate(0, win, table)
    for copy in los:
        copy.wait_recv()
    tabulate(2, win, table)
    to_scalar.wait()

    def tile_body(t, _):
        fetch(t, idx, table, chosen)
        gram(t, chosen, rinv, vals, start, force, scale)
        return 0

    lax.fori_loop(0, ROWS, tile_body, 0)
    own.wait()
    for copy in cs:
        copy.wait_recv()

    flat_cells = cells.reshape(64 * ROWS, 128)
    flat_done = done.reshape(64 * ROWS, 128)
    outs = []
    each = ROWS // PARTS
    for part in range(PARTS):
        t0 = part * each
        zq = newton([pack(start, t0 + 4 * i) for i in range(each // 4)])
        for i in range(each // 4):
            for j in range(2):
                transform_pair(
                    t0 + 4 * i + 2 * j,
                    zq[i][:, 128 * j : 128 * j + 128],
                    force,
                    scale,
                    flat_cells,
                    flat_done,
                )
        rows = pl.ds(t0, each)
        mine = pl.ds(pl.multiple_of(128 * me, 128), 128)
        for i in range(1, MEM):
            to = (me + i) % MEM
            outs.append(
                remote(
                    done.at[pl.ds(KM * to, KM), rows, :],
                    out.at[:, rows, mine],
                    a_send.at[part * MEM + i],
                    a_recv.at[part * MEM + i],
                    (to, sp),
                )
            )
            outs[-1].start()
        last = pltpu.make_async_copy(
            done.at[pl.ds(KM * me, KM), rows, :], out.at[:, rows, mine], local_sem.at[3 + part]
        )
        last.start()
        outs.append(last)
    for copy in ys + zs + los + his + cs:
        copy.wait_send()
    for copy in outs:
        copy.wait()


def on_device(ensemble, spreading, zonal, meridional, ocean, obs_loc, obs_value, obs_sigma, tile_obs):
    vm, dma = pltpu.VMEM, pltpu.SemaphoreType.DMA
    return pl.pallas_call(
        kernel,
        out_shape=jax.ShapeDtypeStruct((KM, ROWS, COLS), f32),
        in_specs=[pl.BlockSpec(memory_space=pl.ANY)] * 9,
        out_specs=pl.BlockSpec(memory_space=pltpu.VMEM),
        scratch_shapes=[
            vm((KM, ROWS, COLS), f32), vm((ROWS, COLS), f32), vm((ROWS, COLS), f32),
            vm((ROWS, COLS), f32), vm((ROWS, COLS), i32),
            vm((3, 16, 128), i32), vm((3, 16, 128), f32), vm((3, 16, 128), f32),
            vm((ROWS, 16, 256), i32), vm((32, 128), i32), pltpu.SMEM((32, 128), i32),
            vm((2, 2 * KM, COLS), f32), vm((2, 4, COLS), f32),
            vm((2 * KM, COLS), f32), vm((4, COLS), f32), vm((2 * KM, COLS), f32), vm((4, COLS), f32),
            vm((KM, ROWS, COLS), f32), vm((8, 8, 128), f32), vm((3, MEM, 8, 8, 128), f32),
            vm((32, 128), f32), vm((32, 128), f32), vm((3 * OBS, 128), f32), vm((256, 128), f32),
            vm((16, 64, 128), f32), vm((16, 128), f32), vm((16, 128), f32),
            vm((64, ROWS, 128), f32), vm((64, ROWS, 128), f32),
            dma((6,)), dma((9,)), dma((4,)), dma((4,)), dma((7,)), dma((7,)), dma((8,)), dma((8,)),
            dma((16,)), dma((16,)), dma((16,)), dma((16,)), dma((MEM,)), dma((MEM,)),
            dma((PARTS * MEM,)), dma((PARTS * MEM,)), dma((3 + PARTS,)),
        ],
        compiler_params=pltpu.CompilerParams(
            collective_id=0, has_side_effects=True, vmem_limit_bytes=40 << 20
        ),
    )(
        ensemble, spreading, zonal, meridional, ocean,
        obs_loc.reshape(SPACE, 16, 128), obs_value.reshape(SPACE, 16, 128),
        obs_sigma.reshape(SPACE, 16, 128), tile_obs,
    )


def solution(mesh):
    in_specs = (
        P("member", "space", None),
        P("space", None),
        P("space", None),
        P("space", None),
        P("space", None),
        P(),
        P(),
        P(),
        P("space", None, None),
    )
    return jax.shard_map(
        on_device,
        mesh=mesh,
        in_specs=in_specs,
        out_specs=P("member", "space", None),
        check_vma=False,
    )
```

time: 265 us -> 93.5 us (0.35)
  the two profiles are of different devices: /device:TPU:135 before, /device:TPU:48 now
where the time goes in v1:
time: 93.5 us; the launch traced here: 93.2 us
  Pallas kernels  83.9 us (90%)
  local copies, waits for them, and re-layouts  9.25 us (10%)
    pallas_call x1, Pallas kernels, on_device(): pl.pallas_call(kernel, out_shape=jax.ShapeDtypeStruct((KM, ROWS, COLS), f...  83.9 us
    unnamed x19, local copies, waits for them, and re-layouts  9.25 us

profile of v1, /device:TPU:48, one launch (start us, length us, event | category | flops | bytes accessed | tf_op | source)
XLA Modules:
  0.0 93.2 jit_solution(14300792680249685851)
XLA Ops:
  0.0 0.0 copy-start
  0.0 1.0 %copy-done = f32[4,16,2048]{2,1,0:T(8,128)S(1)} copy-done((f32[4,16,2048]{2,1,0:T(8,128)S(1)}, f32[4,16,2048]{2,1,0:T(8,128)}, u32[]{:S(2)}) %copy-start) | copy-done | bytes 524312
  1.0 0.0 copy-start.1
  1.0 0.9 %copy-done.1 = s32[65536]{0:T(1024)S(1)} copy-done((s32[65536]{0:T(1024)S(1)}, s32[65536]{0:T(1024)}, u32[]{:S(2)}) %copy-start.1) | copy-done | bytes 262168
  2.0 0.0 copy-start.2
  2.0 0.9 %copy-done.2 = f32[65536]{0:T(1024)S(1)} copy-done((f32[65536]{0:T(1024)S(1)}, f32[65536]{0:T(1024)}, u32[]{:S(2)}) %copy-start.2) | copy-done | bytes 262168
  2.9 0.0 copy-start.3
  2.9 0.9 %copy-done.3 = f32[65536]{0:T(1024)S(1)} copy-done((f32[65536]{0:T(1024)S(1)}, f32[65536]{0:T(1024)}, u32[]{:S(2)}) %copy-start.3) | copy-done | bytes 262168
  3.9 0.0 copy-start.4
  3.9 0.9 %copy-done.4 = s32[16,16,256]{2,1,0:T(8,128)S(1)} copy-done((s32[16,16,256]{2,1,0:T(8,128)S(1)}, s32[16,16,256]{2,1,0:T(8,128)}, u32[]{:S(2)}) %copy-start.4) | copy-done | bytes 262168
  4.8 0.0 copy-start.5
  4.8 0.9 copy-done.5
  5.7 0.0 copy-start.6
  5.8 0.9 copy-done.6
  6.7 0.0 copy-start.7
  6.7 0.9 copy-done.7
  7.6 0.0 copy-start.8
  7.6 0.9 copy-done.8
  8.5 83.9 %shard_map.91 = f32[4,16,2048]{2,1,0:T(8,128)S(1)} custom-call(f32[4,16,2048]{2,1,0:T(8,128)S(1)} %copy-done, f32[16,2048]{1,0:T(8,128)S(1)} %copy-done.5, f32[16,2048]{1,0:T(8,128)S(1)} %copy-done.6, f32[16,2048]{1,0:T(8,128)S(1)} %copy-done.7, s32[16,2048]{1,0:T(8,128)S(1)} %copy-done.8, s32[32,16,128]{2,1,0:T(8,128)S(1)} %bitcast.3, ...), custom_call_target="tpu_custom_call" | custom-call | tf_op jit(solution)/shard_map/pallas_call | solution.py:455
  92.4 0.8 copy.11
Async XLA Ops:
  0.0 1.0 %copy-start = (f32[4,16,2048]{2,1,0:T(8,128)S(1)}, f32[4,16,2048]{2,1,0:T(8,128)}, u32[]{:S(2)}) copy-start(f32[4,16,2048]{2,1,0:T(8,128)} %ens_h.1) | copy-start | bytes 1572868
  1.0 0.9 %copy-start.1 = (s32[65536]{0:T(1024)S(1)}, s32[65536]{0:T(1024)}, u32[]{:S(2)}) copy-start(s32[65536]{0:T(1024)} %param.14) | copy-start | bytes 786436
  2.0 0.9 %copy-start.2 = (f32[65536]{0:T(1024)S(1)}, f32[65536]{0:T(1024)}, u32[]{:S(2)}) copy-start(f32[65536]{0:T(1024)} %param.15) | copy-start | bytes 786436
  2.9 0.9 %copy-start.3 = (f32[65536]{0:T(1024)S(1)}, f32[65536]{0:T(1024)}, u32[]{:S(2)}) copy-start(f32[65536]{0:T(1024)} %param.16) | copy-start | bytes 786436
  3.9 0.9 %copy-start.4 = (s32[16,16,256]{2,1,0:T(8,128)S(1)}, s32[16,16,256]{2,1,0:T(8,128)}, u32[]{:S(2)}) copy-start(s32[16,16,256]{2,1,0:T(8,128)} %tile_h.1) | copy-start | bytes 786436
  4.8 0.9 copy-start.5
  5.7 0.9 copy-start.6
  6.7 0.9 copy-start.7
  7.6 0.9 copy-start.8
